TPU v7x, 32 devices: a whole 2x2x4 slice. The times are simulated.
32 devices in a mesh: row: 8 (over z, x), col: 4 (over y, core).
Axes of the slice: x: 2, y: 2, z: 4, core: 2. Of those that a mesh axis runs over, the one named last changes fastest.
Arguments:
- adjoints: bfloat16 [512, 16, 200], P(('row', 'col')), may hold values from -6 to 6
- jac_blocks: bfloat16 [8, 4, 128, 200, 200], P('row', 'col'), may hold values from -0.4375 to 0.4375
- jac_rows: int32 [8, 4, 128], P('row', 'col'), may hold values from 0 to 63, as said below
- jac_cols: int32 [8, 4, 128], P('row', 'col'), may hold values from 0 to 127, as said below
- tile_count: int32 [8, 4], P('row', 'col'), may hold values from 32 to 128, as said below
Outputs:
- transposed: bfloat16 [512, 16, 200], P('col')
Inputs may be any that keep to these rules, and one draw needn't show every extreme that they name: `jac_rows`: row faces within a tile; both ends are named by some slot. `jac_cols`: column faces within a tile; both ends are named by some slot. `tile_count`: slots at or above the count are padding and are ignored; some tile has exactly 128 live slots.
All inputs are finite; a program needn't handle non-finite values.
Results may differ from a plain program's by a relative error of at most 0.001.
Values may be sent and summed in bfloat16 or wider, within the bound.
A program may use at most 64 MiB of HBM per device.

v0:
```python
import jax
import jax.numpy as jnp
from jax import lax
from jax.sharding import PartitionSpec as P


def add_columns(selector, products):
    return jnp.einsum(
        "cs,ske->cke",
        selector,
        products,
        preferred_element_type=jnp.float32,
        precision=lax.Precision.HIGHEST,
    )


def on_device(adjoints, jac_blocks, jac_rows, jac_cols, tile_count):
    row_block = lax.all_gather(adjoints, "col", axis=0, tiled=True)
    blocks = jac_blocks[0, 0]
    slot_rows = jac_rows[0, 0]
    slot_cols = jac_cols[0, 0]
    live_count = tile_count[0, 0]
    slot_count = slot_rows.shape[0]
    faces_here = adjoints.shape[0]
    column_count = faces_here * lax.axis_size("row")
    picked = jnp.take(row_block, slot_rows, axis=0)
    products = jnp.einsum("skd,sde->ske", picked, blocks, preferred_element_type=jnp.float32)
    live_slot = jnp.arange(slot_count, dtype=jnp.int32) < live_count
    matches = live_slot[None, :] & (
        slot_cols[None, :] == jnp.arange(column_count, dtype=jnp.int32)[:, None]
    )
    partial_value = add_columns(matches.astype(jnp.float32), products)
    summed = lax.psum(partial_value, "row")
    return summed.astype(jnp.bfloat16)


def solution(mesh):
    placed = (
        P(("row", "col"), None, None),
        P("row", "col", None, None, None),
        P("row", "col", None),
        P("row", "col", None),
        P("row", "col"),
    )
    return jax.shard_map(
        on_device, mesh=mesh, in_specs=placed, out_specs=P("col", None, None), check_vma=False
    )
```

profile of v0, /device:TPU:0, one launch (start us, length us, event | category | flops | bytes accessed | tf_op | source)
XLA Modules:
  0.0 123.3 jit_solution(11922159399008281259)
XLA Ops:
  0.0 0.0 copy-start
  0.0 0.0 copy-start.2
  0.0 19.1 %copy.6 = bf16[128,200,200]{2,1,0:T(8,128)(2,1)} copy(bf16[128,200,200]{0,2,1:T(8,128)(2,1)} %bitcast.14) | data formatting | bytes 20480000 | tf_op jit(solution)/shard_map/squeeze | solution.py:19
  19.1 0.0 copy-done
  19.1 8.6 %all_gather.3 = bf16[64,16,200]{2,1,0:T(8,128)(2,1)S(1)} all-gather(bf16[16,16,200]{2,1,0:T(8,128)(2,1)S(1)} %copy-done), channel_id=1, replica_groups=mesh['row'=8,'col'=4] {'col'}, dimensions={0}, use_global_device_ids=true | all-gather | bytes 512000 | tf_op jit(solution)/shard_map/all_gather | solution.py:18
  27.7 0.0 copy-done.2
  27.7 0.6 gather_fusion
  28.4 6.7 %fusion = f32[128,16,200]{2,1,0:T(8,128)S(1)} fusion(bf16[128,200,200]{2,1,0:T(8,128)(2,1)} %copy.6, bf16[128,16,200]{2,1,0:T(8,128)(2,1)S(1)} %gather_fusion, pred[128]{0:T(512)(128)(4,1)S(1)} %compare_and_fusion), kind=kOutput, calls=%fused_computation.1 | convolution fusion | flops 164249600 | bytes 12697728 | tf_op jit(solution)/shard_map/skd,sde->ske/dot_general | solution.py:27
  35.1 0.0 copy-start.1
  35.1 1.8 %copy.7 = f32[128,16,200]{0,2,1:T(8,128)} copy(f32[128,16,200]{2,1,0:T(8,128)S(1)} %fusion) | data formatting | bytes 3276800 | tf_op jit(solution)/shard_map/skd,sde->ske/dot_general | solution.py:27
  37.6 0.0 copy-done.1
  37.6 2.3 %fusion.5 = f32[128,3200]{0,1:S(1)} fusion(f32[128,3200]{0,1:T(8,128)} %bitcast.15, s32[128]{0:T(128)S(1)} %bitcast.17, pred[128]{0:T(512)(128)(4,1)S(1)} %iota_compare_fusion.1), kind=kOutput, calls=%fused_computation.7 | convolution fusion | flops 629178368 | bytes 3277440
  39.9 83.4 %all-reduce.1 = bf16[128,16,200]{0,2,1:T(8,128)(2,1)} all-reduce(f32[128,16,200]{0,2,1:T(8,128)S(1)} %bitcast.16), channel_id=1, replica_groups=mesh['row'=8,'col'=4] {'row'}, use_global_device_ids=true, to_apply=%region_0.1 | all-reduce | flops 409600 | bytes 2457600 | tf_op jit(solution)/shard_map/psum | solution.py:33
  (4 shorter events, 0.0 us)
Async XLA Ops:
  0.0 19.1 %copy-start = (bf16[16,16,200]{2,1,0:T(8,128)(2,1)S(1)}, bf16[16,16,200]{2,1,0:T(8,128)(2,1)}, u32[]{:S(2)}) copy-start(bf16[16,16,200]{2,1,0:T(8,128)(2,1)} %param.5) | copy-start | bytes 307204
  0.0 27.7 %copy-start.2 = (s32[1,1,128]{2,1,0:T(1,128)S(1)}, s32[1,1,128]{2,1,0:T(1,128)}, u32[]{:S(2)}) copy-start(s32[1,1,128]{2,1,0:T(1,128)} %param.7) | copy-start | bytes 1540
  35.1 2.5 %copy-start.1 = (s32[1,1,128]{2,1,0:T(1,128)S(1)}, s32[1,1,128]{2,1,0:T(1,128)}, u32[]{:S(2)}) copy-start(s32[1,1,128]{2,1,0:T(1,128)} %param.8) | copy-start | bytes 1540
where the time goes:
time: 124 us; the launch traced here: 123 us
  blocking collectives  92 us (74%)
  local copies, waits for them, and re-layouts  21.5 us (17%)
  matrix products  9 us (7%)
    psum x1, blocking collectives, on_device(): summed = lax.psum(partial_value, 'row')  83.4 us
    squeeze x1, local copies, waits for them, and re-layouts, on_device(): blocks = jac_blocks[0, 0]  19.1 us
    all_gather x1, blocking collectives, on_device(): row_block = lax.all_gather(adjoints, 'col', axis=0, tiled=True)  8.64 us
    dot_general x1, matrix products, on_device(): jnp.einsum('skd,sde->ske', picked, blocks, preferred_element_type=jnp.flo...  6.7 us

commit v1 on v0

v1 whole, which is shorter than its diff:
```python
import functools

import jax
import jax.numpy as jnp
from jax import lax
from jax.experimental import pallas as pl
from jax.experimental.pallas import tpu as pltpu
from jax.sharding import PartitionSpec as P

MESH = pl.DeviceIdType.MESH
D_STEP = 8
E_CUTS = (0, 48, 96, 144)


def bit_count(n):
    return n.bit_length() - 1


def flip(index, bit):
    size = 2**bit
    return index + size - 2 * size * (index // size % 2)


class Flow:
    def __init__(self, index, base, group, e0, e1, order, n, me, refs):
        self.index, self.base, self.group, self.e0, self.e1 = index, base, group, e0, e1
        self.order, self.n, self.me, self.refs = order, n, me, refs
        self.off = 0
        self.length = n
        self.slot = 0
        self.stage = 0
        self.history = []
        self.sent = []
        self.pending = None

    def copy(self, src, dst, bit):
        refs = self.refs
        made = pltpu.make_async_remote_copy(
            src_ref=src,
            dst_ref=dst,
            send_sem=refs["send"].at[self.index, self.stage],
            recv_sem=refs["recv"].at[self.index, self.stage],
            device_id={"row": flip(self.me, bit)},
            device_id_type=MESH,
        )
        made.start()
        self.sent.append(made)
        self.pending = made

    def step(self):
        refs, rounds = self.refs, len(self.order)
        acc, land, whole = refs["acc"], refs["land"], refs["whole"]
        if self.stage > 2 * rounds:
            return
        e0, e1 = self.e0, self.e1
        e_end = -(-e1 // 16) * 16
        if self.stage:
            self.pending.wait_recv()
            if self.stage <= rounds:
                for i in range(self.length):
                    at = self.base + self.off + i
                    acc[at, e0:e1, :] = (
                        acc[at, e0:e1, :] + land[self.group, self.slot + i, e0:e1, :]
                    )
                self.slot += self.length
        if self.stage < rounds:
            bit = self.order[self.stage]
            half = self.length // 2
            mine = self.me // 2**bit % 2
            self.history.append((bit, self.off, self.length))
            there = self.base + self.off + (1 - mine) * half
            self.copy(
                acc.at[pl.ds(there, half), pl.ds(e0, e1 - e0), :],
                land.at[self.group, pl.ds(self.slot, half), pl.ds(e0, e1 - e0), :],
                bit,
            )
            self.off = self.off + mine * half
            self.length = half
        elif self.stage < 2 * rounds:
            if self.stage == rounds:
                value = acc[self.base + self.off, e0:e1, :]
                if e_end > e1:
                    tail = jnp.zeros((e_end - e1, value.shape[1]), jnp.float32)
                    value = jnp.concatenate([value, tail], axis=0)
                whole[self.base + self.off, e0:e_end, :] = value.astype(jnp.bfloat16)
            else:
                _, self.off, self.length = self.history.pop()
            bit = self.history[-1][0]
            part = whole.at[
                pl.ds(self.base + self.off, self.length), pl.ds(e0, e_end - e0), :
            ]
            self.copy(part, part, bit)
        self.stage += 1


def kernel(
    n_row, n_col,
    adj_ref, blocks_ref, rows_ref, cols_ref, count_ref, out_ref,
    adj_all, adj_wide, picked, block_buf, factor, acc, land, whole,
    block_sem, adj_send, adj_recv, send, recv,
):
    row, col = lax.axis_index("row"), lax.axis_index("col")
    row_bits, col_bits = bit_count(n_row), bit_count(n_col)
    faces, functionals, dofs = adj_ref.shape
    slots = rows_ref.shape[1]
    columns = out_ref.shape[2]
    row_faces = faces * n_col

    fetch = pltpu.make_async_copy(blocks_ref, block_buf, block_sem)
    fetch.start()

    barrier = pltpu.get_barrier_semaphore()
    for bit in range(row_bits):
        pl.semaphore_signal(barrier, inc=1, device_id={"row": flip(row, bit)}, device_id_type=MESH)
    for bit in range(col_bits):
        pl.semaphore_signal(barrier, inc=1, device_id={"col": flip(col, bit)}, device_id_type=MESH)
    pl.semaphore_wait(barrier, row_bits + col_bits)

    adj_all[pl.ds(col * faces, faces)] = adj_ref[...]
    sends = []
    for number, bit in enumerate(reversed(range(col_bits))):
        copies = []
        stride = 2 ** (bit + 1)
        for i in range(2**number):
            shard = col % stride + i * stride
            part = adj_all.at[pl.ds(shard * faces, faces)]
            made = pltpu.make_async_remote_copy(
                src_ref=part,
                dst_ref=part,
                send_sem=adj_send.at[2**number - 1 + i],
                recv_sem=adj_recv.at[2**number - 1 + i],
                device_id={"col": flip(col, bit)},
                device_id_type=MESH,
            )
            made.start()
            copies.append(made)
        for made in copies:
            made.wait_recv()
        sends += copies

    wide = adj_all[...].astype(jnp.float32).reshape(row_faces * functionals, dofs)
    pieces = [(at, min(dofs - at, 128)) for at in range(0, dofs, 128)]
    for i, (at, size) in enumerate(pieces):
        adj_wide[i, :, :size] = wide[:, at : at + size]
    chosen = (
        lax.broadcasted_iota(jnp.int32, (row_faces, slots), 0) == rows_ref[...]
    ).astype(jnp.float32).astype(jnp.bfloat16)
    for k in range(functionals):
        for i, (at, size) in enumerate(pieces):
            rows_k = adj_wide.at[i][pl.ds(k, row_faces, stride=functionals), :]
            found = lax.dot_general(
                rows_k[:, :size].astype(jnp.bfloat16),
                chosen,
                (((0,), (0,)), ((), ())),
                preferred_element_type=jnp.float32,
            )
            picked[pl.ds(k * dofs + at, size), :] = found
    live = lax.broadcasted_iota(jnp.int32, (columns, slots), 1) < count_ref[0, 0]
    named = lax.broadcasted_iota(jnp.int32, (columns, slots), 0) == cols_ref[...]
    selector = (live & named).astype(jnp.float32).astype(jnp.bfloat16)
    fetch.wait()

    def pair(k0):
        acc[k0] = jnp.zeros((dofs, columns), jnp.float32)
        acc[k0 + 1] = jnp.zeros((dofs, columns), jnp.float32)

        def some(step, _):
            d0 = pl.multiple_of(step * D_STEP, D_STEP)
            left = jnp.concatenate([block_buf[d0 + i] for i in range(D_STEP)], axis=1)
            for side in range(2):
                values = picked[pl.ds((k0 + side) * dofs + d0, D_STEP), :]
                for i in range(D_STEP):
                    wide = jnp.broadcast_to(values[i : i + 1, :], (16, slots)).astype(jnp.bfloat16)
                    tiled = jnp.concatenate([wide] * (columns // 16), axis=0)
                    factor[pl.ds(side * columns, columns), pl.ds(i * slots, slots)] = tiled * selector
            product = lax.dot_general(
                left, factor[...], (((1,), (1,)), ((), ())), preferred_element_type=jnp.float32
            )
            acc[k0] += product[:, :columns]
            acc[k0 + 1] += product[:, columns:]
            return 0

        lax.fori_loop(0, dofs // D_STEP, some, 0)

    refs = {"acc": acc, "land": land, "whole": whole, "send": send, "recv": recv}
    groups = functionals // n_row
    flows = []
    for group in range(groups):
        for at in range(0, n_row, 2):
            pair(group * n_row + at)
            for flow in flows:
                flow.step()
        fresh = []
        for i, e0 in enumerate(E_CUTS):
            e1 = E_CUTS[i + 1] if i + 1 < len(E_CUTS) else dofs
            order = list(range(row_bits))
            if i == 0:
                order[0], order[1] = order[1], order[0]
            fresh.append(
                Flow(len(flows) + i, group * n_row, group, e0, e1, order, n_row, row, refs)
            )
        for flow in fresh:
            flow.step()
        flows += fresh
    for _ in range(2 * row_bits):
        for flow in flows:
            flow.step()
    out_ref[...] = whole[:, :dofs, :]
    for flow in flows:
        for made in flow.sent:
            made.wait_send()
    for made in sends:
        made.wait_send()


def on_device(n_row, n_col, adjoints, jac_blocks, jac_rows, jac_cols, tile_count):
    faces, functionals, dofs = adjoints.shape
    slots = jac_rows.shape[-1]
    columns = faces * n_row
    row_faces = faces * n_col
    groups = functionals // n_row
    n_flows = groups * len(E_CUTS)
    rounds = bit_count(n_row)
    padded = -(-dofs // 16) * 16
    blocks = jnp.transpose(jac_blocks[0, 0], (1, 2, 0))
    vmem = pl.BlockSpec(memory_space=pltpu.VMEM)
    out = pl.pallas_call(
        functools.partial(kernel, n_row, n_col),
        out_shape=jax.ShapeDtypeStruct((functionals, dofs, columns), jnp.bfloat16),
        in_specs=[
            vmem,
            pl.BlockSpec(memory_space=pl.ANY),
            vmem,
            vmem,
            pl.BlockSpec(memory_space=pltpu.SMEM),
        ],
        out_specs=vmem,
        scratch_shapes=[
            pltpu.VMEM((row_faces, functionals, dofs), jnp.bfloat16),
            pltpu.VMEM((-(-dofs // 128), row_faces * functionals, 128), jnp.float32),
            pltpu.VMEM((functionals * dofs, slots), jnp.float32),
            pltpu.VMEM((dofs, dofs, slots), jnp.bfloat16),
            pltpu.VMEM((2 * columns, D_STEP * slots), jnp.bfloat16),
            pltpu.VMEM((functionals, dofs, columns), jnp.float32),
            pltpu.VMEM((groups, n_row - 1, dofs, columns), jnp.float32),
            pltpu.VMEM((functionals, padded, columns), jnp.bfloat16),
            pltpu.SemaphoreType.DMA,
            pltpu.SemaphoreType.DMA((n_col - 1,)),
            pltpu.SemaphoreType.DMA((n_col - 1,)),
            pltpu.SemaphoreType.DMA((n_flows, 2 * rounds)),
            pltpu.SemaphoreType.DMA((n_flows, 2 * rounds)),
        ],
        compiler_params=pltpu.CompilerParams(
            collective_id=0, has_side_effects=True, vmem_limit_bytes=48 * 2**20
        ),
    )(adjoints, blocks, jac_rows[0], jac_cols[0], tile_count)
    return jnp.transpose(out, (2, 0, 1))


def solution(mesh):
    placed = (
        P(("row", "col"), None, None),
        P("row", "col", None, None, None),
        P("row", "col", None),
        P("row", "col", None),
        P("row", "col"),
    )
    return jax.shard_map(
        functools.partial(on_device, mesh.shape["row"], mesh.shape["col"]),
        mesh=mesh,
        in_specs=placed,
        out_specs=P("col", None, None),
        check_vma=False,
    )
```

time: 124 us -> 116 us (0.935)
  Pallas kernels: 0 us -> 112 us
  blocking collectives: 92 us -> 0 us
  local copies, waits for them, and re-layouts: 21.5 us -> 3.1 us
  matrix products: 9 us -> 0 us
    pallas_call x0 -> x1, Pallas kernels: none -> 112 us  [on_device(): pl.pallas_call(functools.partial(kernel, n_row, n_col), out_shape=jax.Sha...]
    psum x1 -> x0, blocking collectives: 83.4 us -> none  [on_device(): summed = lax.psum(partial_value, 'row')]
    squeeze x1 -> x0, local copies, waits for them, and re-layouts: 19.1 us -> none  [on_device(): blocks = jac_blocks[0, 0]]
    all_gather x1 -> x0, blocking collectives: 8.64 us -> none  [on_device(): row_block = lax.all_gather(adjoints, 'col', axis=0, tiled=True)]
    dot_general x1 -> x0, matrix products: 6.7 us -> none  [on_device(): jnp.einsum('skd,sde->ske', picked, blocks, preferred_element_type=jnp.flo...]
    unnamed x6 -> x7, local copies, waits for them, and re-layouts: 0.01 us -> 3.1 us
    unnamed x1 -> x0, matrix products: 2.3 us -> none
    dot_general x1 -> x0, local copies, waits for them, and re-layouts: 1.8 us -> none  [on_device(): jnp.einsum('skd,sde->ske', picked, blocks, preferred_element_type=jnp.flo...]
where the time goes in v1:
time: 116 us
  Pallas kernels  112 us (97%)
  local copies, waits for them, and re-layouts  3.1 us (3%)
    pallas_call x1, Pallas kernels, on_device(): pl.pallas_call(functools.partial(kernel, n_row, n_col), out_shape=jax.Sha...  112 us
    unnamed x7, local copies, waits for them, and re-layouts  3.1 us

profile of v1, /device:TPU:0, one launch (start us, length us, event | category | flops | bytes accessed | tf_op | source)
XLA Modules:
  0.0 115.7 jit_solution(270313999729056075)
XLA Ops:
  0.7 0.0 copy-start
  0.7 0.9 copy-done
  1.6 0.0 copy-start.1
  1.6 0.7 copy-done.1
  2.2 0.0 copy-start.2
  2.2 0.7 copy-done.2
  2.9 111.9 %shard_map.55 = bf16[16,200,128]{2,1,0:T(8,128)(2,1)S(1)} custom-call(bf16[16,16,200]{2,1,0:T(8,128)(2,1)S(1)} %copy-done, bf16[200,200,128]{2,1,0:T(8,128)(2,1)} %bitcast.9, s32[1,128]{1,0:T(1,128)S(1)} %bitcast.7, s32[1,128]{1,0:T(1,128)S(1)} %bitcast.8, s32[1,1]{1,0:T(1,128)S(6)} %copy.7.count_ref), custom_call_target="tpu_custom_call" | custom-call | tf_op jit(solution)/shard_map/pallas_call | solution.py:227
  114.8 0.9 copy.8
Async XLA Ops:
  0.7 0.9 copy-start
  1.6 0.7 copy-start.1
  2.2 0.7 copy-start.2

commit v2 on v1

--- a/solution.py
+++ b/solution.py
@@ -8,8 +8,9 @@
 from jax.sharding import PartitionSpec as P
 
 MESH = pl.DeviceIdType.MESH
-D_STEP = 8
-E_CUTS = (0, 48, 96, 144)
+D_STEP = 40
+E_CUTS = (0, 48)
+TOGETHER = 4
 
 
 def bit_count(n):
@@ -53,7 +54,6 @@
         if self.stage > 2 * rounds:
             return
         e0, e1 = self.e0, self.e1
-        e_end = -(-e1 // 16) * 16
         if self.stage:
             self.pending.wait_recv()
             if self.stage <= rounds:
@@ -79,15 +79,12 @@
         elif self.stage < 2 * rounds:
             if self.stage == rounds:
                 value = acc[self.base + self.off, e0:e1, :]
-                if e_end > e1:
-                    tail = jnp.zeros((e_end - e1, value.shape[1]), jnp.float32)
-                    value = jnp.concatenate([value, tail], axis=0)
-                whole[self.base + self.off, e0:e_end, :] = value.astype(jnp.bfloat16)
+                whole[self.base + self.off, e0:e1, :] = value.astype(jnp.bfloat16)
             else:
                 _, self.off, self.length = self.history.pop()
             bit = self.history[-1][0]
             part = whole.at[
-                pl.ds(self.base + self.off, self.length), pl.ds(e0, e_end - e0), :
+                pl.ds(self.base + self.off, self.length), pl.ds(e0, e1 - e0), :
             ]
             self.copy(part, part, bit)
         self.stage += 1
@@ -160,9 +157,12 @@
     selector = (live & named).astype(jnp.float32).astype(jnp.bfloat16)
     fetch.wait()
 
+    parts = n_row // TOGETHER
+    rows = acc.shape[1]
+    cuts = [(p, p * rows, min(rows, dofs - p * rows)) for p in range(parts)]
+
     def pair(k0):
-        acc[k0] = jnp.zeros((dofs, columns), jnp.float32)
-        acc[k0 + 1] = jnp.zeros((dofs, columns), jnp.float32)
+        acc[pl.ds(k0 * parts, 2 * parts)] = jnp.zeros((2 * parts, rows, columns), jnp.float32)
 
         def some(step, _):
             d0 = pl.multiple_of(step * D_STEP, D_STEP)
@@ -176,23 +176,25 @@
             product = lax.dot_general(
                 left, factor[...], (((1,), (1,)), ((), ())), preferred_element_type=jnp.float32
             )
-            acc[k0] += product[:, :columns]
-            acc[k0 + 1] += product[:, columns:]
+            for side in range(2):
+                for p, at, size in cuts:
+                    acc[(k0 + side) * parts + p, :size, :] += product[
+                        at : at + size, side * columns : (side + 1) * columns
+                    ]
             return 0
 
         lax.fori_loop(0, dofs // D_STEP, some, 0)
 
     refs = {"acc": acc, "land": land, "whole": whole, "send": send, "recv": recv}
-    groups = functionals // n_row
     flows = []
-    for group in range(groups):
-        for at in range(0, n_row, 2):
-            pair(group * n_row + at)
+    for group in range(functionals // TOGETHER):
+        for at in range(0, TOGETHER, 2):
+            pair(group * TOGETHER + at)
             for flow in flows:
                 flow.step()
         fresh = []
         for i, e0 in enumerate(E_CUTS):
-            e1 = E_CUTS[i + 1] if i + 1 < len(E_CUTS) else dofs
+            e1 = E_CUTS[i + 1] if i + 1 < len(E_CUTS) else rows
             order = list(range(row_bits))
             if i == 0:
                 order[0], order[1] = order[1], order[0]
@@ -205,7 +207,9 @@
     for _ in range(2 * row_bits):
         for flow in flows:
             flow.step()
-    out_ref[...] = whole[:, :dofs, :]
+    for k in range(functionals):
+        for p, at, size in cuts:
+            out_ref[k, pl.ds(at, size), :] = whole[k * parts + p, :size, :]
     for flow in flows:
         for made in flow.sent:
             made.wait_send()
@@ -218,10 +222,11 @@
     slots = jac_rows.shape[-1]
     columns = faces * n_row
     row_faces = faces * n_col
-    groups = functionals // n_row
+    groups = functionals // TOGETHER
+    parts = n_row // TOGETHER
     n_flows = groups * len(E_CUTS)
     rounds = bit_count(n_row)
-    padded = -(-dofs // 16) * 16
+    rows = -(-dofs // (16 * parts)) * 16
     blocks = jnp.transpose(jac_blocks[0, 0], (1, 2, 0))
     vmem = pl.BlockSpec(memory_space=pltpu.VMEM)
     out = pl.pallas_call(
@@ -241,9 +246,9 @@
             pltpu.VMEM((functionals * dofs, slots), jnp.float32),
             pltpu.VMEM((dofs, dofs, slots), jnp.bfloat16),
             pltpu.VMEM((2 * columns, D_STEP * slots), jnp.bfloat16),
-            pltpu.VMEM((functionals, dofs, columns), jnp.float32),
-            pltpu.VMEM((groups, n_row - 1, dofs, columns), jnp.float32),
-            pltpu.VMEM((functionals, padded, columns), jnp.bfloat16),
+            pltpu.VMEM((functionals * parts, rows, columns), jnp.float32),
+            pltpu.VMEM((groups, n_row - 1, rows, columns), jnp.float32),
+            pltpu.VMEM((functionals * parts, rows, columns), jnp.bfloat16),
             pltpu.SemaphoreType.DMA,
             pltpu.SemaphoreType.DMA((n_col - 1,)),
             pltpu.SemaphoreType.DMA((n_col - 1,)),

time: 116 us -> 82.2 us (0.71)
  Pallas kernels: 112 us -> 78.2 us
    pallas_call x1, Pallas kernels: 112 us -> 78.2 us  [on_device(): pl.pallas_call(functools.partial(kernel, n_row, n_col), out_shape=jax.Sha...]
where the time goes in v2:
time: 82.2 us; the launch traced here: 82 us
  Pallas kernels  78.2 us (95%)
  local copies, waits for them, and re-layouts  3.1 us (4%)
    pallas_call x1, Pallas kernels, on_device(): pl.pallas_call(functools.partial(kernel, n_row, n_col), out_shape=jax.Sha...  78.2 us
    unnamed x7, local copies, waits for them, and re-layouts  3.1 us

profile of v2, /device:TPU:0, one launch (start us, length us, event | category | flops | bytes accessed | tf_op | source)
XLA Modules:
  0.0 82.0 jit_solution(16585501043316235500)
XLA Ops:
  0.7 0.0 copy-start
  0.7 0.9 %copy-done = bf16[16,16,200]{2,1,0:T(8,128)(2,1)S(1)} copy-done((bf16[16,16,200]{2,1,0:T(8,128)(2,1)S(1)}, bf16[16,16,200]{2,1,0:T(8,128)(2,1)}, u32[]{:S(2)}) %copy-start) | copy-done | bytes 102424
  1.6 0.0 copy-start.1
  1.6 0.7 copy-done.1
  2.2 0.0 copy-start.2
  2.2 0.7 copy-done.2
  2.9 78.2 %shard_map.55 = bf16[16,200,128]{2,1,0:T(8,128)(2,1)S(1)} custom-call(bf16[16,16,200]{2,1,0:T(8,128)(2,1)S(1)} %copy-done, bf16[200,200,128]{2,1,0:T(8,128)(2,1)} %bitcast.9, s32[1,128]{1,0:T(1,128)S(1)} %bitcast.7, s32[1,128]{1,0:T(1,128)S(1)} %bitcast.8, s32[1,1]{1,0:T(1,128)S(6)} %copy.7.count_ref), custom_call_target="tpu_custom_call" | custom-call | tf_op jit(solution)/shard_map/pallas_call | solution.py:232
  81.1 0.9 %copy.8 = bf16[128,16,200]{0,2,1:T(8,128)(2,1)} copy(bf16[128,16,200]{0,2,1:T(8,128)(2,1)S(1)} %bitcast.6) | data formatting | bytes 1638400
Async XLA Ops:
  0.7 0.9 %copy-start = (bf16[16,16,200]{2,1,0:T(8,128)(2,1)S(1)}, bf16[16,16,200]{2,1,0:T(8,128)(2,1)}, u32[]{:S(2)}) copy-start(bf16[16,16,200]{2,1,0:T(8,128)(2,1)} %adj_ref.1) | copy-start | bytes 307204
  1.6 0.7 copy-start.1
  2.2 0.7 copy-start.2

commit v3 on v2

--- a/solution.py
+++ b/solution.py
@@ -190,8 +190,9 @@
     for group in range(functionals // TOGETHER):
         for at in range(0, TOGETHER, 2):
             pair(group * TOGETHER + at)
-            for flow in flows:
-                flow.step()
+            if at + 2 < TOGETHER:
+                for flow in flows:
+                    flow.step()
         fresh = []
         for i, e0 in enumerate(E_CUTS):
             e1 = E_CUTS[i + 1] if i + 1 < len(E_CUTS) else rows
@@ -202,6 +203,8 @@
                 Flow(len(flows) + i, group * n_row, group, e0, e1, order, n_row, row, refs)
             )
         for flow in fresh:
+            flow.step()
+        for flow in flows:
             flow.step()
         flows += fresh
     for _ in range(2 * row_bits):

time: 82.2 us -> 82.1 us (level)
  no operation moved by 1% of the time
where the time goes in v3:
time: 82.1 us; the launch traced here: 82 us
  Pallas kernels  78.2 us (95%)
  local copies, waits for them, and re-layouts  3.1 us (4%)
    pallas_call x1, Pallas kernels, on_device(): pl.pallas_call(functools.partial(kernel, n_row, n_col), out_shape=jax.Sha...  78.2 us
    unnamed x7, local copies, waits for them, and re-layouts  3.1 us

profile of v3, /device:TPU:0, one launch (start us, length us, event | category | flops | bytes accessed | tf_op | source)
XLA Modules:
  0.0 82.0 jit_solution(16093996387125579076)
XLA Ops:
  0.7 0.0 copy-start
  0.7 0.9 %copy-done = bf16[16,16,200]{2,1,0:T(8,128)(2,1)S(1)} copy-done((bf16[16,16,200]{2,1,0:T(8,128)(2,1)S(1)}, bf16[16,16,200]{2,1,0:T(8,128)(2,1)}, u32[]{:S(2)}) %copy-start) | copy-done | bytes 102424
  1.6 0.0 copy-start.1
  1.6 0.7 copy-done.1
  2.2 0.0 copy-start.2
  2.2 0.7 copy-done.2
  2.9 78.2 %shard_map.55 = bf16[16,200,128]{2,1,0:T(8,128)(2,1)S(1)} custom-call(bf16[16,16,200]{2,1,0:T(8,128)(2,1)S(1)} %copy-done, bf16[200,200,128]{2,1,0:T(8,128)(2,1)} %bitcast.9, s32[1,128]{1,0:T(1,128)S(1)} %bitcast.7, s32[1,128]{1,0:T(1,128)S(1)} %bitcast.8, s32[1,1]{1,0:T(1,128)S(6)} %copy.7.count_ref), custom_call_target="tpu_custom_call" | custom-call | tf_op jit(solution)/shard_map/pallas_call | solution.py:235
  81.1 0.9 %copy.8 = bf16[128,16,200]{0,2,1:T(8,128)(2,1)} copy(bf16[128,16,200]{0,2,1:T(8,128)(2,1)S(1)} %bitcast.6) | data formatting | bytes 1638400
Async XLA Ops:
  0.7 0.9 %copy-start = (bf16[16,16,200]{2,1,0:T(8,128)(2,1)S(1)}, bf16[16,16,200]{2,1,0:T(8,128)(2,1)}, u32[]{:S(2)}) copy-start(bf16[16,16,200]{2,1,0:T(8,128)(2,1)} %adj_ref.1) | copy-start | bytes 307204
  1.6 0.7 copy-start.1
  2.2 0.7 copy-start.2
